TPU v7x, 32 devices: a whole 2x2x4 slice. The times are simulated.
32 devices in a mesh: ma: 8 (over z, x), ao: 4 (over y, core).
Axes of the slice: x: 2, y: 2, z: 4, core: 2. Of those that a mesh axis runs over, the one named last changes fastest.
Arguments:
- truth_table: bfloat16 [4, 512, 512, 128], P('ao', 'ma'), may hold values from -1 to 1, as said below
- pair_list: int32 [4], replicated, may hold values from 0 to 3, as said below
Outputs:
- cross_corr: float32 [4, 512, 512, 128], P('ao', 'ma')
Inputs may be any that keep to these rules, and one draw needn't show every extreme that they name: `truth_table`: every entry is +1 or -1. `pair_list`: each output's partner is another output, and every output is the partner of exactly one output.
All inputs are finite; a program needn't handle non-finite values.
Results may differ from a plain program's by a relative error of at most 0.0003.
Values sent between devices are 32-bit elements; how exact they have to be, the bound alone decides.
A program may use at most 192 MiB of HBM per device.

v0:
```python
import jax
import jax.numpy as jnp
from jax import lax
from jax.sharding import PartitionSpec as P


def sylvester(length):
    index_row = jnp.arange(length, dtype=jnp.int32)
    shared = jnp.bitwise_and(index_row[:, None], index_row[None, :])
    ones_count = jnp.zeros((length, length), jnp.int32)
    for position in range(length.bit_length() - 1):
        ones_count = ones_count + jnp.bitwise_and(jnp.right_shift(shared, position), 1)
    return (1 - 2 * (ones_count % 2)).astype(jnp.float32)


def apply_low(field, h_low):
    return jnp.einsum("abj,jc->abc", field, h_low, precision=lax.Precision.HIGHEST)


def apply_mid(field, h_mid):
    return jnp.einsum("bj,ajc->abc", h_mid, field, precision=lax.Precision.HIGHEST)


def apply_high(field, h_high, factor):
    return jnp.einsum("ai,ibc->abc", h_high, field, precision=lax.Precision.HIGHEST) * factor


def signs_low(table, h_low_half):
    return jnp.einsum("abj,jc->abc", table, h_low_half, preferred_element_type=jnp.float32)


def signs_mid(field, h_mid_half):
    return jnp.einsum("bj,ajc->abc", h_mid_half, field, preferred_element_type=jnp.float32)


def partner_gathered(spectrum, pair_list):
    mine = lax.axis_index("ao")
    mate = pair_list[mine]
    piece = lax.all_gather(spectrum[None], "ao", axis=0, tiled=True)
    start = jnp.int32(0)
    count = piece.shape[0]
    offset = jnp.clip(mate, 0, count - 1)
    chosen = lax.dynamic_index_in_dim(piece, offset, 0, keepdims=False)
    found = jnp.logical_and(mate >= start, mate < start + count)
    mates = jnp.where(found, chosen, jnp.zeros_like(spectrum))
    return spectrum * mates


def pair_product(spectrum, pair_list):
    return partner_gathered(spectrum, pair_list)


def body(truth_table, pair_list):
    table = truth_table[0]
    rows_here = table.shape[0]
    mid_len = table.shape[1]
    low_len = table.shape[2]
    high_len = rows_here * lax.axis_size("ma")
    factor = 1.0 / jnp.sqrt(jnp.float32(high_len * mid_len * low_len))
    h_high = sylvester(high_len)
    h_mid = sylvester(mid_len)
    h_low = sylvester(low_len)

    def high_step(field):
        return apply_high(field, h_high, factor)

    first_pass = signs_low(table, h_low.astype(jnp.bfloat16)).astype(jnp.bfloat16)
    partial_spec = signs_mid(first_pass, h_mid.astype(jnp.bfloat16))
    spectrum = high_step(
        lax.all_to_all(partial_spec, "ma", split_axis=1, concat_axis=0, tiled=True)
    )
    spectrum = lax.all_to_all(spectrum, "ma", split_axis=0, concat_axis=1, tiled=True)
    product = pair_product(spectrum, pair_list)
    product = apply_mid(apply_low(product, h_low), h_mid)
    mixed = high_step(lax.all_to_all(product, "ma", split_axis=1, concat_axis=0, tiled=True))
    result = lax.all_to_all(mixed, "ma", split_axis=0, concat_axis=1, tiled=True)
    return result[None]


def solution(mesh):
    return jax.shard_map(
        body,
        mesh=mesh,
        in_specs=(P("ao", "ma", None, None), P()),
        out_specs=P("ao", "ma", None, None),
        check_vma=False,
    )
```

profile of v0, /device:TPU:0, one launch (start us, length us, event | category | flops | bytes accessed | tf_op | source)
XLA Modules:
  0.0 2102.0 jit_solution(368012756062145836)
XLA Ops:
  6.5 0.0 all-gather.2.cloned.1.call-start
  6.5 13.9 convolution_bitcast_fusion.1
  20.5 16.6 copy.24
  37.0 370.1 %all_to_all.69 = f32[64,512,128]{2,0,1:T(8,128)S(1)} all-to-all(f32[64,512,128]{2,0,1:T(8,128)} %copy.24), channel_id=1, replica_groups=mesh['ma'=8,'ao'=4] {'ma'}, dimensions={1} | all-to-all | bytes 33554432 | tf_op jit(solution)/shard_map/all_to_all | solution.py:70
  407.1 1.7 copy.26
  408.8 32.4 %convolution_multiply_fusion.1 = f32[512,64,128]{2,0,1:T(8,128)S(1)} fusion(f32[512,64,128]{2,0,1:T(8,128)S(1)} %bitcast.58), kind=kOutput, calls=%fused_computation.5 | convolution fusion | flops 25784745984 | bytes 33554432 | tf_op jit(solution)/shard_map/ai,ibc->abc/dot_general | solution.py:25
  441.2 18.1 copy.27
  459.3 366.6 %all_to_all.70 = f32[512,64,128]{2,1,0:T(8,128)S(1)} all-to-all(f32[512,64,128]{2,1,0:T(8,128)S(1)} %copy.27), channel_id=1, replica_groups=mesh['ma'=8,'ao'=4] {'ma'}, dimensions={0} | all-to-all | bytes 33554432 | tf_op jit(solution)/shard_map/all_to_all | solution.py:72
  825.9 6.2 copy.28
  832.1 0.0 copy-start
  832.1 0.0 all-gather.2.cloned.1.call-update
  832.2 0.6 copy-done
  832.8 0.6 dynamic_slice.7
  835.3 388.0 %all-gather.2.cloned.1.call-done = f32[4,64,512,128]{3,2,1,0:T(8,128)} async-done(((f32[1,64,512,128]{3,2,1,0:T(8,128)}), f32[4,64,512,128]{3,2,1,0:T(8,128)}) %all-gather.2.cloned.1.call-update) | async-done | bytes 67108880 | tf_op jit(solution)/shard_map/all_gather | solution.py:39
  1223.3 24.5 %fusion = f32[64,512,128]{1,2,0:T(8,128)} fusion(f32[64,512,128]{2,1,0:T(8,128)} %bitcast.57, f32[4,64,512,128]{3,2,1,0:T(8,128)} %all-gather.2.cloned.1.call-done, s32[]{:T(128)} %bitcast.16, pred[]{:T(512)} %bitcast.13), kind=kOutput, calls=%fused_computation.1 | convolution fusion | flops 6451412992 | bytes 50332672 | tf_op jit(solution)/shard_map/abj,jc->abc/dot_general | solution.py:17
  1247.8 37.6 %convolution_bitcast_fusion = f32[64,512,128]{1,2,0:T(8,128)} fusion(f32[64,512,128]{1,2,0:T(8,128)} %fusion), kind=kOutput, calls=%fused_computation.6 | convolution fusion | flops 25780551680 | bytes 33554432 | tf_op jit(solution)/shard_map/bj,ajc->abc/dot_general | solution.py:21
  1285.4 16.6 copy.31
  1302.0 368.7 %all_to_all.71 = f32[64,512,128]{2,0,1:T(8,128)S(1)} all-to-all(f32[64,512,128]{2,0,1:T(8,128)} %copy.31), channel_id=1, replica_groups=mesh['ma'=8,'ao'=4] {'ma'}, dimensions={1} | all-to-all | bytes 33554432 | tf_op jit(solution)/shard_map/all_to_all | solution.py:75
  1670.7 1.7 copy.33
  1672.4 31.9 %convolution_multiply_fusion = f32[512,64,128]{2,0,1:T(8,128)S(1)} fusion(f32[512,64,128]{2,0,1:T(8,128)S(1)} %bitcast.59), kind=kOutput, calls=%fused_computation.4 | convolution fusion | flops 25784745984 | bytes 33554432 | tf_op jit(solution)/shard_map/ai,ibc->abc/dot_general | solution.py:25
  1704.3 18.1 copy.34
  1722.4 366.3 %all_to_all.72 = f32[512,64,128]{2,1,0:T(8,128)S(1)} all-to-all(f32[512,64,128]{2,1,0:T(8,128)S(1)} %copy.34), channel_id=1, replica_groups=mesh['ma'=8,'ao'=4] {'ma'}, dimensions={0} | all-to-all | bytes 33554432 | tf_op jit(solution)/shard_map/all_to_all | solution.py:76
  2088.7 6.2 copy.35
Async XLA Ops:
  6.5 1216.8 %all-gather.2.cloned.1.call-start = ((), (), s32[]{:S(2)}) async-start(), calls=%async_computation.4 | async-start | bytes 83886080 | tf_op jit(solution)/shard_map/all_gather | solution.py:39
  832.1 0.7 copy-start
Sparse Core Ops, SparseCore 0:
  832.3 390.9 all-gather.1
where the time goes:
time: 2110 us; the launch traced here: 2100 us
  blocking collectives  1470 us (70%)
  waiting for transfers between devices  388 us (18%)
  matrix products  140 us (7%)
  local copies, waits for them, and re-layouts  86.4 us (4%)
    all_gather x1, waiting for transfers between devices, partner_gathered(): piece = lax.all_gather(spectrum[None], 'ao', axis=0, tiled=True)  388 us
    all_to_all x1, blocking collectives, body(): lax.all_to_all(partial_spec, 'ma', split_axis=1, concat_axis=0, tiled=True)  370 us
    all_to_all x1, blocking collectives, body(): lax.all_to_all(product, 'ma', split_axis=1, concat_axis=0, tiled=True)  369 us
    all_to_all x1, blocking collectives, body(): lax.all_to_all(spectrum, 'ma', split_axis=0, concat_axis=1, tiled=True)  367 us
    all_to_all x1, blocking collectives, body(): lax.all_to_all(mixed, 'ma', split_axis=0, concat_axis=1, tiled=True)  366 us
    dot_general x2, matrix products, apply_high(): jnp.einsum('ai,ibc->abc', h_high, field, precision=lax.Precision.HIGHEST)  64.3 us
  transfers between devices with their start and end apart: 1, of which 1 were waited for; matrix products, arithmetic and copies ran while one was open for 0% of the time, Pallas kernels for 0%

commit v1 on v0

--- a/solution.py
+++ b/solution.py
@@ -2,6 +2,24 @@
 import jax.numpy as jnp
 from jax import lax
 from jax.sharding import PartitionSpec as P
+
+
+def ring_gather(shard, axis, dim):
+    ways, here, step = (lax.axis_size(axis), lax.axis_index(axis), shard.shape[dim])
+    dims = [n * ways if d == dim else n for d, n in enumerate(shard.shape)]
+    full = lax.dynamic_update_slice_in_dim(
+        jnp.zeros(dims, shard.dtype), shard, here * step, axis=dim
+    )
+    going_up = going_down = shard
+    for far in range(1, ways // 2 + 1):
+        going_up = lax.ppermute(going_up, axis, [(d, (d + 1) % ways) for d in range(ways)])
+        full = lax.dynamic_update_slice_in_dim(full, going_up, (here - far) % ways * step, axis=dim)
+        if 2 * far < ways:
+            going_down = lax.ppermute(going_down, axis, [(d, (d - 1) % ways) for d in range(ways)])
+            full = lax.dynamic_update_slice_in_dim(
+                full, going_down, (here + far) % ways * step, axis=dim
+            )
+    return full
 
 
 def sylvester(length):
@@ -36,7 +54,7 @@
 def partner_gathered(spectrum, pair_list):
     mine = lax.axis_index("ao")
     mate = pair_list[mine]
-    piece = lax.all_gather(spectrum[None], "ao", axis=0, tiled=True)
+    piece = ring_gather(spectrum[None], "ao", 0)
     start = jnp.int32(0)
     count = piece.shape[0]
     offset = jnp.clip(mate, 0, count - 1)

time: 2110 us -> 2270 us (1.076)
  waiting for transfers between devices: 388 us -> 484 us
  local copies, waits for them, and re-layouts: 86.4 us -> 153 us
    ppermute x0 -> x3, waiting for transfers between devices: none -> 484 us  [the longest x2 484 us: ring_gather(): lax.ppermute(going_up, axis, [(d, (d + 1) % ways) for d in range(ways)])]
    all_gather x1 -> x0, waiting for transfers between devices: 388 us -> none  [partner_gathered(): piece = lax.all_gather(spectrum[None], 'ao', axis=0, tiled=True)]
    dynamic_update_slice x0 -> x4, local copies, waits for them, and re-layouts: none -> 45.8 us  [the longest x2 22.9 us: ring_gather(): lax.dynamic_update_slice_in_dim(full, going_up, (here - far) % ways * ste...]
  transfers between devices with their start and end apart: 1 -> 3, of which waited for: 1 -> 2; matrix products, arithmetic and copies ran while one was open for 0% -> 2% of each run, Pallas kernels for 0% -> 0%
where the time goes in v1:
time: 2270 us; the launch traced here: 2260 us
  blocking collectives  1470 us (65%)
  waiting for transfers between devices  484 us (21%)
  local copies, waits for them, and re-layouts  153 us (7%)
  matrix products  152 us (7%)
    ppermute x2, waiting for transfers between devices, ring_gather(): lax.ppermute(going_up, axis, [(d, (d + 1) % ways) for d in range(ways)])  484 us
    all_to_all x1, blocking collectives, body(): lax.all_to_all(partial_spec, 'ma', split_axis=1, concat_axis=0, tiled=True)  370 us
    all_to_all x1, blocking collectives, body(): lax.all_to_all(product, 'ma', split_axis=1, concat_axis=0, tiled=True)  367 us
    all_to_all x1, blocking collectives, body(): lax.all_to_all(spectrum, 'ma', split_axis=0, concat_axis=1, tiled=True)  367 us
    all_to_all x1, blocking collectives, body(): lax.all_to_all(mixed, 'ma', split_axis=0, concat_axis=1, tiled=True)  366 us
    dot_general x2, matrix products, apply_high(): jnp.einsum('ai,ibc->abc', h_high, field, precision=lax.Precision.HIGHEST)  76.1 us
  transfers between devices with their start and end apart: 3, of which 2 were waited for; matrix products, arithmetic and copies ran while one was open for 2% of the time, Pallas kernels for 0%

profile of v1, /device:TPU:0, one launch (start us, length us, event | category | flops | bytes accessed | tf_op | source)
XLA Modules:
  0.0 2263.6 jit_solution(17954408230203398667)
XLA Ops:
  0.0 13.9 convolution_bitcast_fusion.1
  13.9 16.6 copy.24
  30.4 370.1 %all_to_all.69 = f32[64,512,128]{2,0,1:T(8,128)S(1)} all-to-all(f32[64,512,128]{2,0,1:T(8,128)} %copy.24), channel_id=1, replica_groups=mesh['ma'=8,'ao'=4] {'ma'}, dimensions={1} | all-to-all | bytes 33554432 | tf_op jit(solution)/shard_map/all_to_all | solution.py:88
  400.6 1.7 copy.26
  402.3 44.1 %convolution_multiply_fusion.1 = f32[512,64,128]{2,0,1:T(8,128)S(1)} fusion(f32[512,64,128]{2,0,1:T(8,128)S(1)} %bitcast.56), kind=kOutput, calls=%fused_computation.5 | convolution fusion | flops 25784745984 | bytes 33554432 | tf_op jit(solution)/shard_map/ai,ibc->abc/dot_general | solution.py:43
  446.5 18.1 copy.27
  464.6 366.6 %all_to_all.70 = f32[512,64,128]{2,1,0:T(8,128)S(1)} all-to-all(f32[512,64,128]{2,1,0:T(8,128)S(1)} %copy.27), channel_id=1, replica_groups=mesh['ma'=8,'ao'=4] {'ma'}, dimensions={0} | all-to-all | bytes 33554432 | tf_op jit(solution)/shard_map/all_to_all | solution.py:90
  831.2 0.0 copy-start
  831.2 6.2 copy.28
  837.4 0.0 collective-permute-start
  837.4 1.7 collective-permute-start.1
  839.2 359.3 %collective-permute-done = f32[1,64,512,128]{3,2,1,0:T(8,128)} collective-permute-done((f32[1,64,512,128]{3,2,1,0:T(8,128)}, f32[1,64,512,128]{3,2,1,0:T(8,128)}, u32[]{:S(2)}, u32[]{:S(2)}) %collective-permute-start) | collective-permute-done | bytes 16777248 | tf_op jit(solution)/shard_map/ppermute | solution.py:15
  1198.4 0.0 collective-permute-start.2
  1198.5 0.0 copy-done
  1198.5 0.6 dynamic_slice.7
  1200.9 21.2 broadcast_in_dim.8
  1222.1 11.5 constant_dynamic-update-slice_fusion.3
  1233.5 11.5 constant_dynamic-update-slice_fusion.2
  1245.0 0.0 collective-permute-done.1
  1245.0 11.5 constant_dynamic-update-slice_fusion.1
  1256.5 125.1 %collective-permute-done.2 = f32[1,64,512,128]{3,2,1,0:T(8,128)} collective-permute-done((f32[1,64,512,128]{3,2,1,0:T(8,128)}, f32[1,64,512,128]{3,2,1,0:T(8,128)}, u32[]{:S(2)}, u32[]{:S(2)}) %collective-permute-start.2) | collective-permute-done | bytes 16777248 | tf_op jit(solution)/shard_map/ppermute | solution.py:15
  1381.5 11.4 constant_dynamic-update-slice_fusion
  1393.0 24.5 %fusion = f32[64,512,128]{1,2,0:T(8,128)} fusion(f32[64,512,128]{2,1,0:T(8,128)} %bitcast.12, f32[4,64,512,128]{3,2,1,0:T(8,128)} %constant_dynamic-update-slice_fusion, s32[]{:T(128)} %bitcast.16, pred[]{:T(512)} %bitcast.13), kind=kOutput, calls=%fused_computation.1 | convolution fusion | flops 6451412992 | bytes 50332672 | tf_op jit(solution)/shard_map/abj,jc->abc/dot_general | solution.py:35
  1417.4 37.6 %convolution_bitcast_fusion = f32[64,512,128]{1,2,0:T(8,128)} fusion(f32[64,512,128]{1,2,0:T(8,128)} %fusion), kind=kOutput, calls=%fused_computation.6 | convolution fusion | flops 25780551680 | bytes 33554432 | tf_op jit(solution)/shard_map/bj,ajc->abc/dot_general | solution.py:39
  1455.1 16.6 copy.31
  1471.6 367.4 %all_to_all.71 = f32[64,512,128]{2,0,1:T(8,128)S(1)} all-to-all(f32[64,512,128]{2,0,1:T(8,128)} %copy.31), channel_id=1, replica_groups=mesh['ma'=8,'ao'=4] {'ma'}, dimensions={1} | all-to-all | bytes 33554432 | tf_op jit(solution)/shard_map/all_to_all | solution.py:93
  1839.0 1.7 copy.33
  1840.7 31.9 %convolution_multiply_fusion = f32[512,64,128]{2,0,1:T(8,128)S(1)} fusion(f32[512,64,128]{2,0,1:T(8,128)S(1)} %bitcast.57), kind=kOutput, calls=%fused_computation.4 | convolution fusion | flops 25784745984 | bytes 33554432 | tf_op jit(solution)/shard_map/ai,ibc->abc/dot_general | solution.py:43
  1872.7 18.1 copy.34
  1890.8 366.3 %all_to_all.72 = f32[512,64,128]{2,1,0:T(8,128)S(1)} all-to-all(f32[512,64,128]{2,1,0:T(8,128)S(1)} %copy.34), channel_id=1, replica_groups=mesh['ma'=8,'ao'=4] {'ma'}, dimensions={0} | all-to-all | bytes 33554432 | tf_op jit(solution)/shard_map/all_to_all | solution.py:94
  2257.0 6.2 copy.35
Async XLA Ops:
  831.2 367.3 %copy-start = (s32[4]{0:T(128)S(1)}, s32[4]{0:T(128)}, u32[]{:S(2)}) copy-start(s32[4]{0:T(128)} %param.3) | copy-start | bytes 52
  837.4 361.0 %collective-permute-start = (f32[1,64,512,128]{3,2,1,0:T(8,128)}, f32[1,64,512,128]{3,2,1,0:T(8,128)}, u32[]{:S(2)}, u32[]{:S(2)}) collective-permute-start(f32[1,64,512,128]{3,2,1,0:T(8,128)} %bitcast.15), channel_id=1, source_target_pairs={{0,1},{1,2},{2,3},{3,0},{4,5},{5,6},{6,7},{7,4},{8,9},{9,10},{10,1... | collective-permute-start | bytes 50331656 | tf_op jit(solution)/shard_map/ppermute | solution.py:15
  837.4 407.6 %collective-permute-start.1 = (f32[1,64,512,128]{3,2,1,0:T(8,128)}, f32[1,64,512,128]{3,2,1,0:T(8,128)}, u32[]{:S(2)}, u32[]{:S(2)}) collective-permute-start(f32[1,64,512,128]{3,2,1,0:T(8,128)} %bitcast.15), channel_id=1, source_target_pairs={{0,3},{1,0},{2,1},{3,2},{4,7},{5,4},{6,5},{7,6},{8,11},{9,8},{10,9... | collective-permute-start | bytes 50331656 | tf_op jit(solution)/shard_map/ppermute | solution.py:18
  1198.4 183.1 %collective-permute-start.2 = (f32[1,64,512,128]{3,2,1,0:T(8,128)}, f32[1,64,512,128]{3,2,1,0:T(8,128)}, u32[]{:S(2)}, u32[]{:S(2)}) collective-permute-start(f32[1,64,512,128]{3,2,1,0:T(8,128)} %collective-permute-done), channel_id=1, source_target_pairs={{0,1},{1,2},{2,3},{3,0},{4,5},{5,6},{6,7},{7,4},{8,9},{9,10},{10,1... | collective-permute-start | bytes 50331656 | tf_op jit(solution)/shard_map/ppermute | solution.py:15
